TPU v7x, 32 devices: a whole 2x2x4 slice. The times are simulated.
32 devices in a mesh: dp: 8 (over y, x, core), seq: 4 (over z).
Axes of the slice: x: 2, y: 2, z: 4, core: 2. Of those that a mesh axis runs over, the one named last changes fastest.
Arguments:
- inputs: bfloat16 [32768, 768], P(('dp', 'seq')), may hold values from -6 to 6
- attn_gain: bfloat16 [768], P('dp'), may hold values from 0.25 to 1.75
- qkv_weight: bfloat16 [768, 2304], P('dp'), may hold values from -0.25 to 0.25
- proj_weight: bfloat16 [768, 768], P('dp'), may hold values from -0.4375 to 0.4375
- mlp_gain: bfloat16 [768], P('dp'), may hold values from 0.25 to 1.75
- in_weight: bfloat16 [768, 2304], P('dp'), may hold values from -0.21875 to 0.21875
- out_weight: bfloat16 [1152, 768], P('dp'), may hold values from -0.25 to 0.25
- cotangent: bfloat16 [32768, 768], P(('dp', 'seq')), may hold values from -12 to 12
Outputs:
- output: bfloat16 [32768, 768], P(('dp', 'seq'))
- input_grad: bfloat16 [32768, 768], P(('dp', 'seq'))
- attn_gain_grad: float32 [768], P('dp')
- qkv_weight_grad: float32 [768, 2304], P('dp')
- proj_weight_grad: float32 [768, 768], P('dp')
- mlp_gain_grad: float32 [768], P('dp')
- in_weight_grad: float32 [768, 2304], P('dp')
- out_weight_grad: float32 [1152, 768], P('dp')
All inputs are finite; a program needn't handle non-finite values.
Results may differ from a plain program's by a relative error of at most 0.02.
Values may be sent and summed in bfloat16 or wider, within the bound.
A program may use at most 128 MiB of HBM per device.

v0:
```python
import jax
import jax.numpy as jnp
from jax import lax
from jax.sharding import PartitionSpec as P

D = 768
HEADS = 12
HEAD_DIM = 64
FF = 1152
WINDOW = 64
QBLOCK = 512
epsilon = 1e-05
theta_base = 10000.0
masked_score = -1e30


def layer_norm(features, gain_vector):
    center = features - jnp.mean(features, -1, keepdims=True)
    spread = jnp.mean(center * center, -1, keepdims=True)
    return center * lax.rsqrt(spread + epsilon) * gain_vector


def rotary_tables(positions, head_width):
    half_width = head_width // 2
    inverse_freq = theta_base ** (-(jnp.arange(half_width, dtype=jnp.float32) * 2.0) / head_width)
    angles = positions[:, None] * inverse_freq[None, :]
    cosine_table = jnp.concatenate([jnp.cos(angles), jnp.cos(angles)], -1)
    sine_table = jnp.concatenate([jnp.sin(angles), jnp.sin(angles)], -1)
    return (cosine_table[:, None, :], sine_table[:, None, :])


def rotate(features, cosine_table, sine_table):
    half_width = features.shape[-1] // 2
    turned = jnp.concatenate([-features[..., half_width:], features[..., :half_width]], -1)
    return features * cosine_table + turned * sine_table


def gated_gelu(up_values):
    gelu_input = up_values[:, :FF]
    gate_half = up_values[:, FF:]
    return jax.nn.gelu(gelu_input, approximate=False) * gate_half


def band_scores(query_block, key_block, first_row, seq_total):
    score_scale = query_block.shape[-1] ** (-0.5)
    key_span = key_block.shape[0]
    scores = (
        jnp.einsum("qhd,khd->hqk", query_block, key_block, preferred_element_type=jnp.float32)
        * score_scale
    )
    query_pos = first_row + jnp.arange(QBLOCK, dtype=jnp.int32)[:, None]
    key_pos = first_row - WINDOW + jnp.arange(key_span, dtype=jnp.int32)[None, :]
    in_band = (jnp.abs(query_pos - key_pos) <= WINDOW) & (key_pos >= 0) & (key_pos < seq_total)
    return jnp.where(in_band[None], scores, masked_score)


def band_forward(queries, key_pad, value_pad, offset, seq_total):
    row_count = queries.shape[0]
    key_span = QBLOCK + 2 * WINDOW

    def one_block(block_index):
        row_start = block_index * QBLOCK
        query_block = lax.dynamic_slice_in_dim(queries, row_start, QBLOCK, 0)
        key_block = lax.dynamic_slice_in_dim(key_pad, row_start, key_span, 0)
        value_block = lax.dynamic_slice_in_dim(value_pad, row_start, key_span, 0)
        scores = band_scores(query_block, key_block, offset + row_start, seq_total)
        row_max = jnp.max(scores, -1, keepdims=True)
        weights = jnp.exp(scores - row_max)
        row_sum = jnp.sum(weights, -1, keepdims=True)
        softmax_low = (weights / row_sum).astype(jnp.bfloat16)
        result = jnp.einsum(
            "hqk,khd->qhd", softmax_low, value_block, preferred_element_type=jnp.float32
        )
        log_sum = jnp.transpose((row_max + jnp.log(row_sum))[:, :, 0])
        return (result, log_sum)

    results, log_sums = lax.map(one_block, jnp.arange(row_count // QBLOCK, dtype=jnp.int32))
    return (results.reshape(queries.shape), log_sums.reshape(row_count, queries.shape[1]))


def band_backward(queries, key_pad, value_pad, grad_out, log_sums, offset, seq_total):
    row_count = queries.shape[0]
    key_span = QBLOCK + 2 * WINDOW
    score_scale = queries.shape[-1] ** (-0.5)

    def one_block(carried, block_index):
        key_grads, value_grads = carried
        row_start = block_index * QBLOCK
        query_block = lax.dynamic_slice_in_dim(queries, row_start, QBLOCK, 0)
        key_block = lax.dynamic_slice_in_dim(key_pad, row_start, key_span, 0)
        value_block = lax.dynamic_slice_in_dim(value_pad, row_start, key_span, 0)
        grad_block = lax.dynamic_slice_in_dim(grad_out, row_start, QBLOCK, 0)
        lse_block = lax.dynamic_slice_in_dim(log_sums, row_start, QBLOCK, 0)
        scores = band_scores(query_block, key_block, offset + row_start, seq_total)
        softmax_out = jnp.exp(scores - jnp.transpose(lse_block)[:, :, None])
        grad_probs = jnp.einsum(
            "qhd,khd->hqk", grad_block, value_block, preferred_element_type=jnp.float32
        )
        inner_sum = jnp.sum(softmax_out * grad_probs, -1, keepdims=True)
        grad_scores = (softmax_out * (grad_probs - inner_sum)).astype(jnp.bfloat16)
        query_grad = (
            jnp.einsum("hqk,khd->qhd", grad_scores, key_block, preferred_element_type=jnp.float32)
            * score_scale
        )
        key_part = (
            jnp.einsum("hqk,qhd->khd", grad_scores, query_block, preferred_element_type=jnp.float32)
            * score_scale
        )
        value_part = jnp.einsum(
            "hqk,qhd->khd",
            softmax_out.astype(jnp.bfloat16),
            grad_block,
            preferred_element_type=jnp.float32,
        )
        key_grads = lax.dynamic_update_slice_in_dim(
            key_grads,
            lax.dynamic_slice_in_dim(key_grads, row_start, key_span, 0) + key_part,
            row_start,
            0,
        )
        value_grads = lax.dynamic_update_slice_in_dim(
            value_grads,
            lax.dynamic_slice_in_dim(value_grads, row_start, key_span, 0) + value_part,
            row_start,
            0,
        )
        return ((key_grads, value_grads), query_grad)

    padded_zero = jnp.zeros(key_pad.shape, jnp.float32)
    carried, query_grads = lax.scan(
        one_block, (padded_zero, padded_zero), jnp.arange(row_count // QBLOCK, dtype=jnp.int32)
    )
    return (query_grads.reshape(queries.shape), carried[0], carried[1])


def shards(inputs, attn_gain, qkv_weight, proj_weight, mlp_gain, in_weight, out_weight, cotangent):
    gathered = (
        lax.all_gather(qkv_weight, "dp", axis=0, tiled=True),
        lax.all_gather(proj_weight, "dp", axis=0, tiled=True),
        lax.all_gather(in_weight, "dp", axis=0, tiled=True),
        lax.all_gather(out_weight, "dp", axis=0, tiled=True),
        lax.all_gather(attn_gain, "dp", axis=0, tiled=True),
        lax.all_gather(mlp_gain, "dp", axis=0, tiled=True),
    )
    qkv_full, proj_full, in_full, out_full, attn_full, mlp_full = gathered
    tokens = inputs.shape[0]
    seq_count = lax.axis_size("seq")
    seq_total = tokens * seq_count
    offset = lax.axis_index("seq") * tokens
    local_heads = HEADS // seq_count
    residual = inputs.astype(jnp.float32)
    normed_one, norm_one_back = jax.vjp(layer_norm, residual, attn_full.astype(jnp.float32))
    normed_low = normed_one.astype(jnp.bfloat16)
    projected = jnp.dot(normed_low, qkv_full, preferred_element_type=jnp.float32)
    positions = (offset + jnp.arange(tokens, dtype=jnp.int32)).astype(jnp.float32)
    cosine_table, sine_table = rotary_tables(positions, HEAD_DIM)

    def turn_pair(raw_pairs):
        return rotate(raw_pairs.reshape(tokens, 2 * HEADS, HEAD_DIM), cosine_table, sine_table)

    turned, turn_back = jax.vjp(turn_pair, projected[:, : 2 * D])
    query_low = turned[:, :HEADS].reshape(tokens, D).astype(jnp.bfloat16)
    key_low = turned[:, HEADS:].reshape(tokens, D).astype(jnp.bfloat16)
    value_low = projected[:, 2 * D :].astype(jnp.bfloat16)
    stacked = jnp.stack([query_low, key_low, value_low], 1)
    by_heads = lax.all_to_all(stacked, "seq", split_axis=2, concat_axis=0, tiled=True)
    head_queries = by_heads[:, 0].reshape(seq_total, local_heads, HEAD_DIM)
    keys_padded = jnp.pad(
        by_heads[:, 1].reshape(seq_total, local_heads, HEAD_DIM), ((WINDOW, WINDOW), (0, 0), (0, 0))
    )
    values_padded = jnp.pad(
        by_heads[:, 2].reshape(seq_total, local_heads, HEAD_DIM), ((WINDOW, WINDOW), (0, 0), (0, 0))
    )
    attended, log_sums = band_forward(head_queries, keys_padded, values_padded, 0, seq_total)
    attended_low = attended.astype(jnp.bfloat16).reshape(seq_total, D // seq_count)
    mixed_low = lax.all_to_all(attended_low, "seq", split_axis=0, concat_axis=1, tiled=True)
    attn_out = jnp.dot(mixed_low, proj_full, preferred_element_type=jnp.float32)
    hidden_state = residual + attn_out
    normed_two, norm_two_back = jax.vjp(layer_norm, hidden_state, mlp_full.astype(jnp.float32))
    normed_two_low = normed_two.astype(jnp.bfloat16)
    up_values = jnp.dot(normed_two_low, in_full, preferred_element_type=jnp.float32)
    gated, gated_back = jax.vjp(gated_gelu, up_values)
    gated_low = gated.astype(jnp.bfloat16)
    result = hidden_state + jnp.dot(gated_low, out_full, preferred_element_type=jnp.float32)
    output = result.astype(jnp.bfloat16)
    grad_result = cotangent.astype(jnp.float32)
    out_grad = jnp.einsum("tf,td->fd", gated_low, cotangent, preferred_element_type=jnp.float32)
    gated_grad = jnp.einsum("td,fd->tf", cotangent, out_full, preferred_element_type=jnp.float32)
    up_grad = gated_back(gated_grad)[0]
    up_low = up_grad.astype(jnp.bfloat16)
    in_grad = jnp.einsum("td,tf->df", normed_two_low, up_low, preferred_element_type=jnp.float32)
    normed_two_grad = jnp.einsum("tf,df->td", up_low, in_full, preferred_element_type=jnp.float32)
    hidden_part, mlp_gain_grad = norm_two_back(normed_two_grad)
    hidden_grad = grad_result + hidden_part
    attn_low = hidden_grad.astype(jnp.bfloat16)
    proj_grad = jnp.einsum("te,td->ed", mixed_low, attn_low, preferred_element_type=jnp.float32)
    mixed_grad = jnp.einsum(
        "td,ed->te", attn_low, proj_full, preferred_element_type=jnp.float32
    ).astype(jnp.bfloat16)
    grad_heads = lax.all_to_all(mixed_grad, "seq", split_axis=1, concat_axis=0, tiled=True)
    grad_heads = grad_heads.reshape(seq_total, local_heads, HEAD_DIM)
    query_grad, key_pad_grad, value_pad_grad = band_backward(
        head_queries, keys_padded, values_padded, grad_heads, log_sums, 0, seq_total
    )
    head_grads = jnp.stack(
        [
            query_grad.reshape(seq_total, D // seq_count),
            key_pad_grad[WINDOW : WINDOW + seq_total].reshape(seq_total, D // seq_count),
            value_pad_grad[WINDOW : WINDOW + seq_total].reshape(seq_total, D // seq_count),
        ],
        1,
    ).astype(jnp.bfloat16)
    token_grads = lax.all_to_all(head_grads, "seq", split_axis=0, concat_axis=2, tiled=True)
    rotated_grad = jnp.concatenate(
        [
            token_grads[:, 0].reshape(tokens, HEADS, HEAD_DIM),
            token_grads[:, 1].reshape(tokens, HEADS, HEAD_DIM),
        ],
        1,
    ).astype(jnp.float32)
    raw_grad = turn_back(rotated_grad)[0]
    proj_in_grad = jnp.concatenate([raw_grad, token_grads[:, 2].astype(jnp.float32)], 1).astype(
        jnp.bfloat16
    )
    qkv_grad = jnp.einsum("td,tf->df", normed_low, proj_in_grad, preferred_element_type=jnp.float32)
    normed_grad = jnp.einsum(
        "tf,df->td", proj_in_grad, qkv_full, preferred_element_type=jnp.float32
    )
    input_part, attn_gain_grad = norm_one_back(normed_grad)
    input_grad = (hidden_grad + input_part).astype(jnp.bfloat16)
    shares = (
        lax.psum_scatter(qkv_grad, "dp", scatter_dimension=0, tiled=True),
        lax.psum_scatter(proj_grad, "dp", scatter_dimension=0, tiled=True),
        lax.psum_scatter(in_grad, "dp", scatter_dimension=0, tiled=True),
        lax.psum_scatter(out_grad, "dp", scatter_dimension=0, tiled=True),
        lax.psum_scatter(attn_gain_grad, "dp", scatter_dimension=0, tiled=True),
        lax.psum_scatter(mlp_gain_grad, "dp", scatter_dimension=0, tiled=True),
    )
    totals = (
        lax.psum(shares[0].astype(jnp.bfloat16), "seq").astype(jnp.float32),
        lax.psum(shares[1].astype(jnp.bfloat16), "seq").astype(jnp.float32),
        lax.psum(shares[2].astype(jnp.bfloat16), "seq").astype(jnp.float32),
        lax.psum(shares[3].astype(jnp.bfloat16), "seq").astype(jnp.float32),
        lax.psum(shares[4].astype(jnp.bfloat16), "seq").astype(jnp.float32),
        lax.psum(shares[5].astype(jnp.bfloat16), "seq").astype(jnp.float32),
    )
    return (output, input_grad, totals[4], totals[0], totals[1], totals[5], totals[2], totals[3])


def solution(mesh):
    in_specs = (
        P(("dp", "seq"), None),
        P("dp"),
        P("dp", None),
        P("dp", None),
        P("dp"),
        P("dp", None),
        P("dp", None),
        P(("dp", "seq"), None),
    )
    out_specs = (
        P(("dp", "seq"), None),
        P(("dp", "seq"), None),
        P("dp"),
        P("dp", None),
        P("dp", None),
        P("dp"),
        P("dp", None),
        P("dp", None),
    )
    return jax.shard_map(shards, mesh=mesh, in_specs=in_specs, out_specs=out_specs, check_vma=False)
```

profile of v0, /device:TPU:0, one launch (start us, length us, event | category | flops | bytes accessed | tf_op | source)
XLA Modules:
  0.0 997.3 jit_solution(2272519886768296588)
XLA Ops:
  11.6 15.3 %all-reduce.11 = (bf16[768]{0:T(1024)(128)(2,1)S(1)}, bf16[768]{0:T(1024)(128)(2,1)S(1)}) all-reduce(bf16[768]{0:T(1024)(128)(2,1)S(1)} %dynamic-update-slice, bf16[768]{0:T(1024)(128)(2,1)S(1)} %dynamic-update-slice.1), channel_id=1, replica_groups=mesh['dp'=8,'seq'=4] {'dp'}, use_global_device_ids=true, to_apply=%add.6 | all-reduce | flops 1536 | bytes 6144
  29.0 17.7 %all-gather.5.cloned.1.call-done = bf16[768,2304]{1,0:T(8,128)(2,1)} async-done(((bf16[96,2304]{1,0:T(8,128)(2,1)}), bf16[768,2304]{1,0:T(8,128)(2,1)}) %all-gather.5.cloned.1.call-update) | async-done | bytes 3538960 | tf_op jit(solution)/shard_map/all_gather | solution.py:138
  46.7 6.2 fusion.81
  56.7 6.6 copy.55
  80.8 11.1 %copy.58 = bf16[1024,3,768]{0,1,2:T(4,128)(2,1)} copy(bf16[1024,3,768]{2,0,1:T(8,128)(2,1)} %pad_maximum_fusion) | data formatting | bytes 9437184 | tf_op jit(solution)/shard_map/stack | solution.py:165
  98.6 137.3 %all-to-all-done = bf16[1024,3,768]{0,1,2:T(4,128)(2,1)} async-done(((bf16[1024,3,768]{0,1,2:T(4,128)(2,1)}), bf16[1024,3,768]{0,1,2:T(4,128)(2,1)}, u32[]{:S(2)}, u32[]{:S(2)}) %all-to-all-start) | async-done | bytes 4718624 | tf_op jit(solution)/shard_map/all_to_all | solution.py:166
  246.6 67.9 %while.30 = (s32[]{:T(128)}, bf16[8,512,3,64]{1,3,2,0:T(8,128)(2,1)}, f32[8,512,3]{1,2,0:T(4,128)}, s32[8]{0:T(128)S(1)}, bf16[4224,3,64]{0,2,1:T(8,128)(2,1)}, ...) while((s32[]{:T(128)}, ...), condition=%wide.region_5.6_spmd, body=%wide.region_2.5_spmd.sunk | while | flops 265094656 | bytes 14252788 | solution.py:77
  332.6 33.3 %all-to-all-done.1 = bf16[4,1024,192]{1,2,0:T(8,128)(2,1)} async-done(((bf16[4,1024,192]{1,2,0:T(8,128)(2,1)}), bf16[4,1024,192]{1,2,0:T(8,128)(2,1)}, u32[]{:S(2)}, u32[]{:S(2)}) %all-to-all-start.1) | async-done | bytes 1572896 | tf_op jit(solution)/shard_map/all_to_all | solution.py:176
  371.3 10.7 %fusion.89 = f32[1024,2304]{1,0:T(8,128)} fusion(bf16[768,2304]{1,0:T(8,128)(2,1)} %all-gather.9.cloned.1.call-done, f32[1024,768]{0,1:T(8,128)} %copy-done.6, f32[768]{0:T(1024)S(1)} %convert_element_type.148, f32[1024]{0:T(1024)S(1)} %fusion.84, f32[1024]{0:T(1024)S(1)} %broadcast_multiply_fusion), kind=kOutput, calls=%fused_computation.152 | convolution fusion | flops 3627024384 | bytes 16133120 | tf_op jit(solution)/shard_map/dot_general | solution.py:181
  382.0 14.9 %fusion.76 = (f32[1024,1152]{1,0:T(8,128)}, f32[1024,1152]{1,0:T(8,128)S(1)}, f32[1024,1152]{1,0:T(8,128)S(1)}) fusion(f32[1024,2304]{1,0:T(8,128)} %fusion.89, bf16[1024,768]{1,0:T(8,128)(2,1)S(1)} %copy-done.15, bf16[1152,768]{1,0:T(8,128)(2,1)} %all-gather.11.cloned.1.call-done), kind=kOutput, calls=%fused_computation.125 | convolution fusion | flops 1888616448 | bytes 22216704 | tf_op jit(solution)/shard_map/td,fd->tf/dot_general | solution.py:188
  400.4 9.0 multiply_reduce_fusion.1
  432.0 11.4 %fusion.77 = f32[768,2304]{1,0:T(8,128)} fusion(f32[1024,1152]{1,0:T(8,128)} %copy-done.9, f32[1024,1152]{1,0:T(8,128)} %get-tuple-element.312, f32[1024,768]{0,1:T(8,128)} %copy-done.6, f32[768]{0:T(1024)S(1)} %convert_element_type.148, f32[1024]{0:T(1024)S(1)} %fusion.84, f32[1024]{0:T(1024)S(1)} %broadcast_multiply_fusion), kind=kOutput, calls=%fused_computation.126 | convolution fusion | flops 3631742976 | bytes 19672064 | tf_op jit(solution)/shard_map/td,tf->df/dot_general | solution.py:191
  443.5 24.9 %all-to-all-done.2 = bf16[1024,4,192]{0,2,1:T(8,128)(2,1)S(1)} async-done(((bf16[1024,4,192]{0,2,1:T(8,128)(2,1)}), bf16[1024,4,192]{0,2,1:T(8,128)(2,1)S(1)}, u32[]{:S(2)}, u32[]{:S(2)}) %all-to-all-start.2) | async-done | bytes 1572896 | tf_op jit(solution)/shard_map/all_to_all | solution.py:200
  479.1 134.9 %while.31 = (s32[]{:T(128)}, f32[4224,3,64]{0,2,1:T(8,128)}, f32[4224,3,64]{0,2,1:T(8,128)}, bf16[8,512,3,64]{1,3,2,0:T(8,128)(2,1)}, s32[8]{0:T(128)S(1)}, /*in...) while((s32[]{:T(128)}, f32[4224,3,64]{0,2,1:T(8,128)}, ...), condition=%wide.region_12.13_spmd, body=%wide.region_10.12_spmd.sunk | while | flops 640099840 | bytes 49803588 | solution.py:130
  624.4 12.8 %copy.67 = bf16[4096,3,192]{2,1,0:T(4,128)(2,1)} copy(bf16[4096,3,192]{0,2,1:T(8,128)(2,1)} %pad_maximum_fusion.1) | data formatting | bytes 9437184 | tf_op jit(solution)/shard_map/stack | solution.py:205
  637.2 190.6 %all_to_all.68 = bf16[4096,3,192]{2,1,0:T(4,128)(2,1)} all-to-all(bf16[4096,3,192]{2,1,0:T(4,128)(2,1)} %copy.67), channel_id=1, replica_groups=mesh['dp'=8,'seq'=4] {'seq'}, dimensions={0} | all-to-all | bytes 9437184 | tf_op jit(solution)/shard_map/all_to_all | solution.py:213
  827.8 12.8 %copy.69 = bf16[1024,3,4,192]{0,3,2,1:T(8,128)(2,1)} copy(bf16[1024,3,4,192]{3,1,0,2:T(4,128)(2,1)} %bitcast.117) | data formatting | bytes 9437184 | tf_op jit(solution)/shard_map/all_to_all | solution.py:213
  848.8 7.7 fusion.72
  857.2 6.7 add_convert_fusion.2
  870.4 8.6 fusion.71
  881.4 38.9 %reduce-scatter.5.cloned.1.call-done = f32[96,2304]{1,0:T(8,128)} async-done(((f32[768,2304]{1,0:T(8,128)}), f32[96,2304]{1,0:T(8,128)}) %reduce-scatter.5.cloned.1.call-update) | async-done | bytes 884752 | tf_op jit(solution)/shard_map/reduce_scatter | solution.py:232
  925.6 13.4 %all-reduce.10 = (bf16[768]{0:T(1024)(128)(2,1)S(1)}, bf16[768]{0:T(1024)(128)(2,1)S(1)}) all-reduce(f32[768]{0:T(1024)S(1)} %get-tuple-element.264, f32[768]{0:T(1024)S(1)} %get-tuple-element.262), channel_id=2, replica_groups=mesh['dp'=8,'seq'=4] {'dp'}, use_global_device_ids=true, to_apply=%region_16.17.clone | all-reduce | flops 1536 | bytes 9216
  939.1 12.3 %all-reduce.12 = (bf16[96]{0:T(256)(128)(2,1)S(1)}, bf16[96]{0:T(256)(128)(2,1)S(1)}) all-reduce(bf16[96]{0:T(256)(128)(2,1)S(1)} %dynamic-slice.9, bf16[96]{0:T(256)(128)(2,1)S(1)} %dynamic-slice.8), channel_id=1, replica_groups=mesh['dp'=8,'seq'=4] {'seq'}, use_global_device_ids=true, to_apply=%region_17.18 | all-reduce | flops 192 | bytes 768 | tf_op jit(solution)/shard_map/psum | solution.py:244
  960.5 23.2 %all-reduce.16.cloned.1.call-done = (bf16[96,2304]{1,0:T(8,128)(2,1)}, bf16[96,768]{1,0:T(8,128)(2,1)}, bf16[96,2304]{1,0:T(8,128)(2,1)}, bf16[144,768]{1,0:T(8,128)(2,1)}) async-done(((bf16[96,2304]{1,0:T(8,128)(2,1)}, bf16[96,768]{1,0:T(8,128)(2,1)}, bf16[96,2304]{1,0:T(8,128)(2,1)}, bf16[144,768]{1,0:T(8,128)(2,1)}), (bf16[96,2304]{1,0:T(8,128)(2,1)}, bf16[96,768]{1,0:T(8,128)(2,1)}, ...) | async-done | bytes 1253392 | tf_op jit(solution)/shard_map/psum | solution.py:240
  (355 shorter events, 345.3 us)
Async XLA Ops:
  7.2 39.5 %all-gather.5.cloned.1.call-start = ((), (), s32[]{:S(2)}) async-start(), calls=%async_computation.8 | async-start | bytes 3981312 | tf_op jit(solution)/shard_map/all_gather | solution.py:138
  9.7 356.2 %copy-start.1 = (bf16[1024,768]{0,1:T(8,128)(2,1)}, bf16[1024,768]{0,1:T(8,128)(2,1)S(1)}, u32[]{:S(2)}) copy-start(bf16[1024,768]{0,1:T(8,128)(2,1)S(1)} %copy.54) | copy-start | bytes 4718596
  26.9 26.0 %copy-start.21 = (f32[768]{0:T(1024)}, f32[768]{0:T(1024)S(1)}, u32[]{:S(2)}) copy-start(f32[768]{0:T(1024)S(1)} %convert_element_type.141) | copy-start | bytes 9220
  28.2 38.7 %copy-start.11 = (f32[1024,64]{0,1:T(8,128)}, f32[1024,64]{0,1:T(8,128)S(1)}, u32[]{:S(2)}) copy-start(f32[1024,64]{0,1:T(8,128)S(1)} %get-tuple-element.346) | copy-start | bytes 786436
  28.5 24.4 %copy-start.19 = (f32[1024]{0:T(1024)}, f32[1024]{0:T(1024)S(1)}, u32[]{:S(2)}) copy-start(f32[1024]{0:T(1024)S(1)} %broadcast_multiply_fusion.1) | copy-start | bytes 12292
  29.0 23.9 %copy-start.25 = (f32[1024]{0:T(1024)}, f32[1024]{0:T(1024)S(1)}, u32[]{:S(2)}) copy-start(f32[1024]{0:T(1024)S(1)} %fusion.70) | copy-start | bytes 12292
  29.0 23.9 %copy-start.23 = (f32[1024]{0:T(1024)}, f32[1024]{0:T(1024)S(1)}, u32[]{:S(2)}) copy-start(f32[1024]{0:T(1024)S(1)} %fusion.83) | copy-start | bytes 12292
  91.9 144.1 %all-to-all-start = ((bf16[1024,3,768]{0,1,2:T(4,128)(2,1)}), bf16[1024,3,768]{0,1,2:T(4,128)(2,1)}, u32[]{:S(2)}, u32[]{:S(2)}) async-start(bf16[1024,3,768]{0,1,2:T(4,128)(2,1)} %copy.58), calls=%async_computation | async-start | bytes 12582912 | tf_op jit(solution)/shard_map/all_to_all | solution.py:166
  97.1 235.5 %all-gather.7.cloned.1.call-start = ((), (), s32[]{:S(2)}) async-start(), calls=%async_computation.9 | async-start | bytes 1327104 | tf_op jit(solution)/shard_map/all_gather | solution.py:139
  97.9 273.4 %all-gather.9.cloned.1.call-start = ((), (), s32[]{:S(2)}) async-start(), calls=%async_computation.10 | async-start | bytes 3981312 | tf_op jit(solution)/shard_map/all_gather | solution.py:140
  324.6 41.3 %all-to-all-start.1 = ((bf16[4,1024,192]{1,2,0:T(8,128)(2,1)}), bf16[4,1024,192]{1,2,0:T(8,128)(2,1)}, u32[]{:S(2)}, u32[]{:S(2)}) async-start(bf16[4,1024,192]{1,2,0:T(8,128)(2,1)} %copy.62), calls=%async_computation.1 | async-start | bytes 3145728 | tf_op jit(solution)/shard_map/all_to_all | solution.py:176
  329.0 53.1 %all-gather.11.cloned.1.call-start = ((), (), s32[]{:S(2)}) async-start(), calls=%async_computation.11 | async-start | bytes 1990656 | tf_op jit(solution)/shard_map/all_gather | solution.py:141
  329.5 537.4 %reduce-scatter.7.cloned.1.call-start = ((), (), s32[]{:S(2)}) async-start(), calls=%async_computation.13 | async-start | bytes 2654208 | tf_op jit(solution)/shard_map/reduce_scatter | solution.py:233
  371.3 10.8 %copy-start.15 = (bf16[1024,768]{1,0:T(8,128)(2,1)S(1)}, bf16[1024,768]{1,0:T(8,128)(2,1)}, u32[]{:S(2)}) copy-start(bf16[1024,768]{1,0:T(8,128)(2,1)} %param.19) | copy-start | bytes 4718596
  382.0 14.9 %copy-start.8 = (f32[1024,2304]{1,0:T(8,128)S(1)}, f32[1024,2304]{1,0:T(8,128)}, u32[]{:S(2)}) copy-start(f32[1024,2304]{1,0:T(8,128)} %fusion.89) | copy-start | bytes 28311556
  400.4 9.0 copy-start.9
  417.3 451.3 %reduce-scatter.11.cloned.1.call-start = ((), (), s32[]{:S(2)}) async-start(), calls=%async_computation.15 | async-start | bytes 3981312 | tf_op jit(solution)/shard_map/reduce_scatter | solution.py:235
  428.4 40.0 %all-to-all-start.2 = ((bf16[1024,4,192]{0,2,1:T(8,128)(2,1)}), bf16[1024,4,192]{0,2,1:T(8,128)(2,1)S(1)}, u32[]{:S(2)}, u32[]{:S(2)}) async-start(bf16[1024,4,192]{0,2,1:T(8,128)(2,1)} %bitcast.135), calls=%async_computation.2 | async-start | bytes 3145728 | tf_op jit(solution)/shard_map/all_to_all | solution.py:200
  431.9 447.2 %reduce-scatter.9.cloned.1.call-start = ((), (), s32[]{:S(2)}) async-start(), calls=%async_computation.14 | async-start | bytes 7962624 | tf_op jit(solution)/shard_map/reduce_scatter | solution.py:234
  443.4 476.9 %reduce-scatter.5.cloned.1.call-start = ((), (), s32[]{:S(2)}) async-start(), calls=%async_computation.12 | async-start | bytes 7962624 | tf_op jit(solution)/shard_map/reduce_scatter | solution.py:232
  856.5 127.2 %all-reduce.16.cloned.1.call-start = ((), (), s32[]{:S(2)}) async-start(), calls=%async_computation.16 | async-start | bytes 2506752 | tf_op jit(solution)/shard_map/psum | solution.py:240
  870.4 8.6 copy-start.26
  922.3 30.1 %copy-start.5 = (bf16[1024,768]{0,1:T(8,128)(2,1)S(1)}, bf16[1024,768]{0,1:T(8,128)(2,1)}, u32[]{:S(2)}) copy-start(bf16[1024,768]{0,1:T(8,128)(2,1)} %copy.64) | copy-start | bytes 4718596
  983.8 5.7 copy-start.18
  (27 other events, 86.4 us)
Sparse Core Ops, SparseCore 0:
  9.9 36.7 all-gather.4
  99.8 24.4 all-gather.6
  126.3 33.9 all-gather.8
  331.4 26.9 all-gather.10
  417.5 40.6 reduce-scatter.6
  461.8 48.0 reduce-scatter.10
  513.9 65.5 reduce-scatter.8
  856.7 63.5 reduce-scatter.4
  923.7 59.9 all-reduce.15
where the time goes:
time: 1010 us; the launch traced here: 997 us
  waiting for transfers between devices  278 us (28%)
  matrix products  244 us (24%)
  blocking collectives  232 us (23%)
  local copies, waits for them, and re-layouts  131 us (13%)
  other arithmetic  72 us (7%)
  between operations  16.2 us (2%)
  starting transfers between devices  14.1 us (1%)
  loops' own time  10.6 us (1%)
    all_to_all x1, blocking collectives, shards(): lax.all_to_all(head_grads, 'seq', split_axis=0, concat_axis=2, tiled=True)  191 us
    all_to_all x1, waiting for transfers between devices, shards(): lax.all_to_all(stacked, 'seq', split_axis=2, concat_axis=0, tiled=True)  137 us
    dot_general x16, matrix products, band_scores(): jnp.einsum('qhd,khd->hqk', query_block, key_block, preferred_element_type...  48.2 us
    reduce_scatter x1, waiting for transfers between devices, shards(): lax.psum_scatter(qkv_grad, 'dp', scatter_dimension=0, tiled=True)  38.9 us
    all_to_all x1, waiting for transfers between devices, shards(): lax.all_to_all(attended_low, 'seq', split_axis=0, concat_axis=1, tiled=True)  33.3 us
    unnamed x2, blocking collectives  28.7 us
    dot_general x8, matrix products, one_block(): jnp.einsum('qhd,khd->hqk', grad_block, value_block, preferred_element_typ...  28.3 us
    dot_general x8, matrix products, one_block(): jnp.einsum('hqk,khd->qhd', softmax_low, value_block, preferred_element_ty...  25.1 us
  transfers between devices with their start and end apart: 12, of which 6 were waited for; matrix products, arithmetic and copies ran while one was open for 35% of the time, Pallas kernels for 0%

commit v1 on v0

--- a/solution.py
+++ b/solution.py
@@ -210,7 +210,19 @@
         ],
         1,
     ).astype(jnp.bfloat16)
-    token_grads = lax.all_to_all(head_grads, "seq", split_axis=0, concat_axis=2, tiled=True)
+    ways, here = (lax.axis_size("seq"), lax.axis_index("seq"))
+    width = head_grads.shape[0] // ways
+    shape = list(head_grads.shape)
+    shape[0] = width
+    height = shape[2]
+    shape[2] = height * ways
+    full = jnp.zeros(shape, head_grads.dtype)
+    for mask in range(ways):
+        part = lax.dynamic_slice_in_dim(head_grads, (here ^ mask) * width, width, axis=0)
+        if mask:
+            part = lax.ppermute(part, "seq", [(d, d ^ mask) for d in range(ways)])
+        full = lax.dynamic_update_slice_in_dim(full, part, (here ^ mask) * height, axis=2)
+    token_grads = full
     rotated_grad = jnp.concatenate(
         [
             token_grads[:, 0].reshape(tokens, HEADS, HEAD_DIM),

time: 1010 us -> 899 us (0.89)
  blocking collectives: 232 us -> 41 us
  waiting for transfers between devices: 278 us -> 375 us
  local copies, waits for them, and re-layouts: 131 us -> 113 us
    all_to_all x1 -> x0, blocking collectives: 191 us -> none  [shards(): lax.all_to_all(head_grads, 'seq', split_axis=0, concat_axis=2, tiled=True)]
    ppermute x0 -> x3, waiting for transfers between devices: none -> 75.1 us  [shards(): part = lax.ppermute(part, 'seq', [(d, d ^ mask) for d in range(ways)])]
    reduce_scatter x1, waiting for transfers between devices: 38.9 us -> 61.4 us  [shards(): lax.psum_scatter(qkv_grad, 'dp', scatter_dimension=0, tiled=True)]
    another operation x2 -> x1, local copies, waits for them, and re-layouts: 13.6 us -> 0.78 us  [shards(): jnp.stack([query_grad.reshape(seq_total, D // seq_count), key_pad_grad[WI...]
    all_to_all x1 -> x0, local copies, waits for them, and re-layouts: 12.8 us -> none  [shards(): lax.all_to_all(head_grads, 'seq', split_axis=0, concat_axis=2, tiled=True)]
  transfers between devices with their start and end apart: 12 -> 15, of which waited for: 6 -> 8; matrix products, arithmetic and copies ran while one was open for 35% -> 38% of each run, Pallas kernels for 0% -> 0%
where the time goes in v1:
time: 899 us; the launch traced here: 888 us
  waiting for transfers between devices  375 us (42%)
  matrix products  245 us (27%)
  local copies, waits for them, and re-layouts  113 us (13%)
  other arithmetic  69.6 us (8%)
  blocking collectives  41 us (5%)
  starting transfers between devices  18.5 us (2%)
  between operations  16.2 us (2%)
  loops' own time  9.62 us (1%)
    all_to_all x1, waiting for transfers between devices, shards(): lax.all_to_all(stacked, 'seq', split_axis=2, concat_axis=0, tiled=True)  137 us
    ppermute x3, waiting for transfers between devices, shards(): part = lax.ppermute(part, 'seq', [(d, d ^ mask) for d in range(ways)])  75.1 us
    reduce_scatter x1, waiting for transfers between devices, shards(): lax.psum_scatter(qkv_grad, 'dp', scatter_dimension=0, tiled=True)  61.4 us
    dot_general x16, matrix products, band_scores(): jnp.einsum('qhd,khd->hqk', query_block, key_block, preferred_element_type...  48.6 us
    all_to_all x1, waiting for transfers between devices, shards(): lax.all_to_all(attended_low, 'seq', split_axis=0, concat_axis=1, tiled=True)  33.3 us
    dot_general x8, matrix products, one_block(): jnp.einsum('qhd,khd->hqk', grad_block, value_block, preferred_element_typ...  28.9 us
    unnamed x2, blocking collectives  28.7 us
    dot_general x8, matrix products, one_block(): jnp.einsum('hqk,khd->qhd', softmax_low, value_block, preferred_element_ty...  25.1 us
  transfers between devices with their start and end apart: 15, of which 8 were waited for; matrix products, arithmetic and copies ran while one was open for 38% of the time, Pallas kernels for 0%

profile of v1, /device:TPU:0, one launch (start us, length us, event | category | flops | bytes accessed | tf_op | source)
XLA Modules:
  0.0 888.0 jit_solution(9546111749362094757)
XLA Ops:
  11.5 15.3 %all-reduce.11 = (bf16[768]{0:T(1024)(128)(2,1)S(1)}, bf16[768]{0:T(1024)(128)(2,1)S(1)}) all-reduce(bf16[768]{0:T(1024)(128)(2,1)S(1)} %dynamic-update-slice, bf16[768]{0:T(1024)(128)(2,1)S(1)} %dynamic-update-slice.1), channel_id=1, replica_groups=mesh['dp'=8,'seq'=4] {'dp'}, use_global_device_ids=true, to_apply=%add.6 | all-reduce | flops 1536 | bytes 6144
  29.0 17.7 %all-gather.5.cloned.1.call-done = bf16[768,2304]{1,0:T(8,128)(2,1)} async-done(((bf16[96,2304]{1,0:T(8,128)(2,1)}), bf16[768,2304]{1,0:T(8,128)(2,1)}) %all-gather.5.cloned.1.call-update) | async-done | bytes 3538960 | tf_op jit(solution)/shard_map/all_gather | solution.py:138
  46.7 6.2 fusion.81
  56.7 6.6 copy.41
  80.7 11.1 %copy.44 = bf16[1024,3,768]{0,1,2:T(4,128)(2,1)} copy(bf16[1024,3,768]{2,0,1:T(8,128)(2,1)} %pad_maximum_fusion) | data formatting | bytes 9437184 | tf_op jit(solution)/shard_map/stack | solution.py:165
  98.6 137.3 %all-to-all-done = bf16[1024,3,768]{0,1,2:T(4,128)(2,1)} async-done(((bf16[1024,3,768]{0,1,2:T(4,128)(2,1)}), bf16[1024,3,768]{0,1,2:T(4,128)(2,1)}, u32[]{:S(2)}, u32[]{:S(2)}) %all-to-all-start) | async-done | bytes 4718624 | tf_op jit(solution)/shard_map/all_to_all | solution.py:166
  246.6 67.9 %while.30 = (s32[]{:T(128)}, bf16[8,512,3,64]{1,3,2,0:T(8,128)(2,1)}, f32[8,512,3]{1,2,0:T(4,128)}, s32[8]{0:T(128)S(1)}, bf16[4224,3,64]{0,2,1:T(8,128)(2,1)}, ...) while((s32[]{:T(128)}, ...), condition=%wide.region_5.6_spmd, body=%wide.region_2.5_spmd.sunk | while | flops 265094656 | bytes 14252788 | solution.py:77
  332.6 33.3 %all-to-all-done.1 = bf16[4,1024,192]{1,2,0:T(8,128)(2,1)} async-done(((bf16[4,1024,192]{1,2,0:T(8,128)(2,1)}), bf16[4,1024,192]{1,2,0:T(8,128)(2,1)}, u32[]{:S(2)}, u32[]{:S(2)}) %all-to-all-start.1) | async-done | bytes 1572896 | tf_op jit(solution)/shard_map/all_to_all | solution.py:176
  371.3 10.7 %fusion.89 = f32[1024,2304]{1,0:T(8,128)} fusion(bf16[768,2304]{1,0:T(8,128)(2,1)} %all-gather.9.cloned.1.call-done, f32[1024,768]{0,1:T(8,128)} %copy-done.6, f32[768]{0:T(1024)S(1)} %convert_element_type.148, f32[1024]{0:T(1024)S(1)} %fusion.84, f32[1024]{0:T(1024)S(1)} %broadcast_multiply_fusion), kind=kOutput, calls=%fused_computation.159 | convolution fusion | flops 3627024384 | bytes 16133120 | tf_op jit(solution)/shard_map/dot_general | solution.py:181
  382.0 14.9 %fusion.76 = (f32[1024,1152]{1,0:T(8,128)}, f32[1024,1152]{1,0:T(8,128)S(1)}, f32[1024,1152]{1,0:T(8,128)S(1)}) fusion(f32[1024,2304]{1,0:T(8,128)} %fusion.89, bf16[1024,768]{1,0:T(8,128)(2,1)S(1)} %copy-done.15, bf16[1152,768]{1,0:T(8,128)(2,1)} %all-gather.11.cloned.1.call-done), kind=kOutput, calls=%fused_computation.125 | convolution fusion | flops 1888616448 | bytes 22216704 | tf_op jit(solution)/shard_map/td,fd->tf/dot_general | solution.py:188
  400.5 9.0 %multiply_reduce_fusion.1 = (f32[768]{0:T(1024)S(1)}, f32[1024]{0:T(1024)S(1)}, f32[1024,768]{0,1:T(8,128)S(1)}) fusion(f32[1024,768]{0,1:T(8,128)S(1)} %copy-done.7, f32[1024]{0:T(1024)S(1)} %fusion.84, f32[1024]{0:T(1024)S(1)} %broadcast_multiply_fusion, f32[768]{0:T(1024)S(1)} %convert_element_type.148, ...), kind=kOutput, calls=%fused_computation.112 | convolution fusion | flops 3634100480 | bytes 19286016 | tf_op jit(solution)/shard_map/tf,df->td/dot_general | solution.py:192
  417.6 5.5 fusion.99
  432.1 11.5 %fusion.77 = f32[768,2304]{1,0:T(8,128)} fusion(f32[1024,1152]{1,0:T(8,128)} %copy-done.9, f32[1024,1152]{1,0:T(8,128)} %get-tuple-element.304, f32[1024,768]{0,1:T(8,128)} %copy-done.6, f32[768]{0:T(1024)S(1)} %convert_element_type.148, f32[1024]{0:T(1024)S(1)} %fusion.84, f32[1024]{0:T(1024)S(1)} %broadcast_multiply_fusion), kind=kOutput, calls=%fused_computation.127 | convolution fusion | flops 3631742976 | bytes 19672064 | tf_op jit(solution)/shard_map/td,tf->df/dot_general | solution.py:191
  443.6 24.8 %all-to-all-done.2 = bf16[1024,4,192]{0,2,1:T(8,128)(2,1)S(1)} async-done(((bf16[1024,4,192]{0,2,1:T(8,128)(2,1)}), bf16[1024,4,192]{0,2,1:T(8,128)(2,1)S(1)}, u32[]{:S(2)}, u32[]{:S(2)}) %all-to-all-start.2) | async-done | bytes 1572896 | tf_op jit(solution)/shard_map/all_to_all | solution.py:200
  479.0 134.3 %while.31 = (s32[]{:T(128)}, f32[4224,3,64]{0,2,1:T(8,128)}, f32[4224,3,64]{0,2,1:T(8,128)}, bf16[8,512,3,64]{1,3,2,0:T(8,128)(2,1)}, s32[8]{0:T(128)S(1)}, /*in...) while((s32[]{:T(128)}, f32[4224,3,64]{0,2,1:T(8,128)}, ...), condition=%wide.region_12.13_spmd, body=%wide.region_10.12_spmd.sunk | while | flops 640099840 | bytes 49803588 | solution.py:130
  631.3 47.7 %collective-permute-done = bf16[1024,3,192]{0,2,1:T(8,128)(2,1)S(1)} collective-permute-done((bf16[1024,3,192]{0,2,1:T(8,128)(2,1)}, bf16[1024,3,192]{0,2,1:T(8,128)(2,1)S(1)}, u32[]{:S(2)}, u32[]{:S(2)}) %collective-permute-start) | collective-permute-done | bytes 1179680 | tf_op jit(solution)/shard_map/ppermute | solution.py:223
  680.0 27.4 %collective-permute-done.1 = bf16[1024,3,192]{0,2,1:T(8,128)(2,1)S(1)} collective-permute-done((bf16[1024,3,192]{0,2,1:T(8,128)(2,1)}, bf16[1024,3,192]{0,2,1:T(8,128)(2,1)S(1)}, u32[]{:S(2)}, u32[]{:S(2)}) %collective-permute-start.1) | collective-permute-done | bytes 1179680 | tf_op jit(solution)/shard_map/ppermute | solution.py:223
  717.9 8.0 fusion.72
  726.6 6.5 add_convert_fusion.2
  737.4 8.5 fusion.71
  749.7 61.4 %reduce-scatter.5.cloned.1.call-done = f32[96,2304]{1,0:T(8,128)} async-done(((f32[768,2304]{1,0:T(8,128)}), f32[96,2304]{1,0:T(8,128)}) %reduce-scatter.5.cloned.1.call-update) | async-done | bytes 884752 | tf_op jit(solution)/shard_map/reduce_scatter | solution.py:244
  816.3 13.4 %all-reduce.10 = (bf16[768]{0:T(1024)(128)(2,1)S(1)}, bf16[768]{0:T(1024)(128)(2,1)S(1)}) all-reduce(f32[768]{0:T(1024)S(1)} %get-tuple-element.256, f32[768]{0:T(1024)S(1)} %get-tuple-element.254), channel_id=2, replica_groups=mesh['dp'=8,'seq'=4] {'dp'}, use_global_device_ids=true, to_apply=%region_16.17.clone | all-reduce | flops 1536 | bytes 9216
  829.8 12.3 %all-reduce.12 = (bf16[96]{0:T(256)(128)(2,1)S(1)}, bf16[96]{0:T(256)(128)(2,1)S(1)}) all-reduce(bf16[96]{0:T(256)(128)(2,1)S(1)} %dynamic-slice.9, bf16[96]{0:T(256)(128)(2,1)S(1)} %dynamic-slice.8), channel_id=1, replica_groups=mesh['dp'=8,'seq'=4] {'seq'}, use_global_device_ids=true, to_apply=%region_17.18 | all-reduce | flops 192 | bytes 768 | tf_op jit(solution)/shard_map/psum | solution.py:256
  851.2 23.3 %all-reduce.16.cloned.1.call-done = (bf16[96,2304]{1,0:T(8,128)(2,1)}, bf16[96,768]{1,0:T(8,128)(2,1)}, bf16[96,2304]{1,0:T(8,128)(2,1)}, bf16[144,768]{1,0:T(8,128)(2,1)}) async-done(((bf16[96,2304]{1,0:T(8,128)(2,1)}, bf16[96,768]{1,0:T(8,128)(2,1)}, bf16[96,2304]{1,0:T(8,128)(2,1)}, bf16[144,768]{1,0:T(8,128)(2,1)}), (bf16[96,2304]{1,0:T(8,128)(2,1)}, bf16[96,768]{1,0:T(8,128)(2,1)}, ...) | async-done | bytes 1253392 | tf_op jit(solution)/shard_map/psum | solution.py:252
  (363 shorter events, 349.9 us)
Async XLA Ops:
  7.2 39.5 %all-gather.5.cloned.1.call-start = ((), (), s32[]{:S(2)}) async-start(), calls=%async_computation.7 | async-start | bytes 3981312 | tf_op jit(solution)/shard_map/all_gather | solution.py:138
  9.7 356.2 %copy-start.1 = (bf16[1024,768]{0,1:T(8,128)(2,1)}, bf16[1024,768]{0,1:T(8,128)(2,1)S(1)}, u32[]{:S(2)}) copy-start(bf16[1024,768]{0,1:T(8,128)(2,1)S(1)} %copy.40) | copy-start | bytes 4718596
  26.9 26.0 %copy-start.21 = (f32[768]{0:T(1024)}, f32[768]{0:T(1024)S(1)}, u32[]{:S(2)}) copy-start(f32[768]{0:T(1024)S(1)} %convert_element_type.141) | copy-start | bytes 9220
  28.2 38.7 %copy-start.11 = (f32[1024,64]{0,1:T(8,128)}, f32[1024,64]{0,1:T(8,128)S(1)}, u32[]{:S(2)}) copy-start(f32[1024,64]{0,1:T(8,128)S(1)} %get-tuple-element.342) | copy-start | bytes 786436
  28.5 24.4 %copy-start.19 = (f32[1024]{0:T(1024)}, f32[1024]{0:T(1024)S(1)}, u32[]{:S(2)}) copy-start(f32[1024]{0:T(1024)S(1)} %broadcast_multiply_fusion.1) | copy-start | bytes 12292
  29.0 23.9 %copy-start.25 = (f32[1024]{0:T(1024)}, f32[1024]{0:T(1024)S(1)}, u32[]{:S(2)}) copy-start(f32[1024]{0:T(1024)S(1)} %fusion.70) | copy-start | bytes 12292
  29.0 23.9 %copy-start.23 = (f32[1024]{0:T(1024)}, f32[1024]{0:T(1024)S(1)}, u32[]{:S(2)}) copy-start(f32[1024]{0:T(1024)S(1)} %fusion.83) | copy-start | bytes 12292
  91.8 144.1 %all-to-all-start = ((bf16[1024,3,768]{0,1,2:T(4,128)(2,1)}), bf16[1024,3,768]{0,1,2:T(4,128)(2,1)}, u32[]{:S(2)}, u32[]{:S(2)}) async-start(bf16[1024,3,768]{0,1,2:T(4,128)(2,1)} %copy.44), calls=%async_computation | async-start | bytes 12582912 | tf_op jit(solution)/shard_map/all_to_all | solution.py:166
  97.1 235.5 %all-gather.7.cloned.1.call-start = ((), (), s32[]{:S(2)}) async-start(), calls=%async_computation.8 | async-start | bytes 1327104 | tf_op jit(solution)/shard_map/all_gather | solution.py:139
  97.8 273.4 %all-gather.9.cloned.1.call-start = ((), (), s32[]{:S(2)}) async-start(), calls=%async_computation.9 | async-start | bytes 3981312 | tf_op jit(solution)/shard_map/all_gather | solution.py:140
  324.6 41.3 %all-to-all-start.1 = ((bf16[4,1024,192]{1,2,0:T(8,128)(2,1)}), bf16[4,1024,192]{1,2,0:T(8,128)(2,1)}, u32[]{:S(2)}, u32[]{:S(2)}) async-start(bf16[4,1024,192]{1,2,0:T(8,128)(2,1)} %copy.48), calls=%async_computation.1 | async-start | bytes 3145728 | tf_op jit(solution)/shard_map/all_to_all | solution.py:176
  329.0 53.0 %all-gather.11.cloned.1.call-start = ((), (), s32[]{:S(2)}) async-start(), calls=%async_computation.10 | async-start | bytes 1990656 | tf_op jit(solution)/shard_map/all_gather | solution.py:141
  329.5 406.2 %reduce-scatter.7.cloned.1.call-start = ((), (), s32[]{:S(2)}) async-start(), calls=%async_computation.12 | async-start | bytes 2654208 | tf_op jit(solution)/shard_map/reduce_scatter | solution.py:245
  371.2 10.8 %copy-start.15 = (bf16[1024,768]{1,0:T(8,128)(2,1)S(1)}, bf16[1024,768]{1,0:T(8,128)(2,1)}, u32[]{:S(2)}) copy-start(bf16[1024,768]{1,0:T(8,128)(2,1)} %param.19) | copy-start | bytes 4718596
  382.0 15.0 %copy-start.8 = (f32[1024,2304]{1,0:T(8,128)S(1)}, f32[1024,2304]{1,0:T(8,128)}, u32[]{:S(2)}) copy-start(f32[1024,2304]{1,0:T(8,128)} %fusion.89) | copy-start | bytes 28311556
  417.5 328.4 %reduce-scatter.11.cloned.1.call-start = ((), (), s32[]{:S(2)}) async-start(), calls=%async_computation.14 | async-start | bytes 3981312 | tf_op jit(solution)/shard_map/reduce_scatter | solution.py:247
  428.4 39.9 %all-to-all-start.2 = ((bf16[1024,4,192]{0,2,1:T(8,128)(2,1)}), bf16[1024,4,192]{0,2,1:T(8,128)(2,1)S(1)}, u32[]{:S(2)}, u32[]{:S(2)}) async-start(bf16[1024,4,192]{0,2,1:T(8,128)(2,1)} %bitcast.128), calls=%async_computation.2 | async-start | bytes 3145728 | tf_op jit(solution)/shard_map/all_to_all | solution.py:200
  432.0 315.7 %reduce-scatter.9.cloned.1.call-start = ((), (), s32[]{:S(2)}) async-start(), calls=%async_computation.13 | async-start | bytes 7962624 | tf_op jit(solution)/shard_map/reduce_scatter | solution.py:246
  443.6 367.5 %reduce-scatter.5.cloned.1.call-start = ((), (), s32[]{:S(2)}) async-start(), calls=%async_computation.11 | async-start | bytes 7962624 | tf_op jit(solution)/shard_map/reduce_scatter | solution.py:244
  626.9 52.1 %collective-permute-start = (bf16[1024,3,192]{0,2,1:T(8,128)(2,1)}, bf16[1024,3,192]{0,2,1:T(8,128)(2,1)S(1)}, u32[]{:S(2)}, u32[]{:S(2)}) collective-permute-start(bf16[1024,3,192]{0,2,1:T(8,128)(2,1)} %get-tuple-element.325), channel_id=1, source_target_pairs={{0,1},{1,0},{2,3},{3,2},{4,5},{5,4},{6,7},{7,6},{8,9},{9,8},{10,11... | collective-permute-start | bytes 3538952 | tf_op jit(solution)/shard_map/ppermute | solution.py:223
  626.9 80.6 %collective-permute-start.1 = (bf16[1024,3,192]{0,2,1:T(8,128)(2,1)}, bf16[1024,3,192]{0,2,1:T(8,128)(2,1)S(1)}, u32[]{:S(2)}, u32[]{:S(2)}) collective-permute-start(bf16[1024,3,192]{0,2,1:T(8,128)(2,1)} %get-tuple-element.324), channel_id=1, source_target_pairs={{0,2},{1,3},{2,0},{3,1},{4,6},{5,7},{6,4},{7,5},{8,10},{9,11},{10,... | collective-permute-start | bytes 3538952 | tf_op jit(solution)/shard_map/ppermute | solution.py:223
  628.9 79.7 %collective-permute-start.2 = (bf16[1024,3,192]{0,2,1:T(8,128)(2,1)}, bf16[1024,3,192]{0,2,1:T(8,128)(2,1)S(1)}, u32[]{:S(2)}, u32[]{:S(2)}) collective-permute-start(bf16[1024,3,192]{0,2,1:T(8,128)(2,1)} %get-tuple-element.323), channel_id=1, source_target_pairs={{0,3},{1,2},{2,1},{3,0},{4,7},{5,6},{6,5},{7,4},{8,11},{9,10},{10,... | collective-permute-start | bytes 3538952 | tf_op jit(solution)/shard_map/ppermute | solution.py:223
  725.9 148.6 %all-reduce.16.cloned.1.call-start = ((), (), s32[]{:S(2)}) async-start(), calls=%async_computation.15 | async-start | bytes 2506752 | tf_op jit(solution)/shard_map/psum | solution.py:252
  813.0 30.1 %copy-start.5 = (bf16[1024,768]{0,1:T(8,128)(2,1)S(1)}, bf16[1024,768]{0,1:T(8,128)(2,1)}, u32[]{:S(2)}) copy-start(bf16[1024,768]{0,1:T(8,128)(2,1)} %copy.50) | copy-start | bytes 4718596
  (30 other events, 109.9 us)
Sparse Core Ops, SparseCore 0:
  9.9 36.7 all-gather.4
  99.8 24.4 all-gather.6
  126.2 33.9 all-gather.8
  331.4 26.9 all-gather.10
  417.6 40.6 reduce-scatter.6
  462.0 48.0 reduce-scatter.10
  514.1 65.5 reduce-scatter.8
  726.0 84.9 reduce-scatter.4
  814.5 59.9 all-reduce.15
